TPU v7x, 32 devices: a whole 2x2x4 slice. The times are simulated.
32 devices in a mesh: seq: 8 (over z, y), chan: 4 (over x, core).
Axes of the slice: x: 2, y: 2, z: 4, core: 2. Of those that a mesh axis runs over, the one named last changes fastest.
Arguments:
- outer_gate: bfloat16 [256, 262144], P('chan', 'seq'), may hold values from -6 to 6
- inner_gate: bfloat16 [256, 262144], P('chan', 'seq'), may hold values from -6 to 6
- signal: bfloat16 [256, 262144], P('chan', 'seq'), may hold values from -6 to 6
- filter_spectrum: float32 [2, 4, 512, 512], P(None, None, 'seq'), may hold values from -6 to 6
- cotangent: bfloat16 [256, 262144], P('chan', 'seq'), may hold values from -6 to 6
Outputs:
- output: bfloat16 [256, 262144], P('chan', 'seq')
- gradient_outer: bfloat16 [256, 262144], P('chan', 'seq')
- gradient_inner: bfloat16 [256, 262144], P('chan', 'seq')
- gradient_signal: bfloat16 [256, 262144], P('chan', 'seq')
- gradient_filter: float32 [2, 4, 512, 512], P(None, None, 'seq')
All inputs are finite; a program needn't handle non-finite values.
Results may differ from a plain program's by a relative error of at most 0.018.
Values may be sent and summed in bfloat16 or wider, within the bound.
A program may use at most 256 MiB of HBM per device.

v0:
```python
import math

import jax
import jax.numpy as jnp
from jax import lax
from jax.sharding import PartitionSpec as P


def wave_tables(factor):
    ordinal = jnp.arange(factor, dtype=jnp.int32)
    phases = ordinal[:, None] * ordinal[None, :] % factor
    angles = phases.astype(jnp.float32) * (2.0 * math.pi / factor)
    return (jnp.cos(angles).astype(jnp.bfloat16), jnp.sin(angles).astype(jnp.bfloat16))


def twist_grid(leading, second, length):
    phases = leading[:, None] * second[None, :] % length
    angles = phases.astype(jnp.float32) * (2.0 * math.pi / length)
    return (jnp.cos(angles), jnp.sin(angles))


def product(operand, pattern, matrix):
    return jnp.einsum(pattern, operand, matrix, preferred_element_type=jnp.float32)


def transform(stacked, spread, collect, tables, location, length):
    cos_table, sin_table = tables
    factor = cos_table.shape[0]
    received = spread(stacked)
    block_size = received.shape[3]
    columns = location * block_size + jnp.arange(block_size, dtype=jnp.int32)
    wave_cos, wave_sin = twist_grid(columns, jnp.arange(factor, dtype=jnp.int32), length)
    sectioned_re = product(received, "ncab,ak->ncbk", cos_table)
    sectioned_im = -product(received, "ncab,ak->ncbk", sin_table)
    twisted = jnp.stack(
        [
            sectioned_re * wave_cos + sectioned_im * wave_sin,
            sectioned_im * wave_cos - sectioned_re * wave_sin,
        ],
        axis=1,
    ).astype(jnp.bfloat16)
    arrived = collect(twisted)
    arrived_re = arrived[:, 0]
    arrived_im = arrived[:, 1]
    spectrum_re = product(arrived_re, "ncbk,bm->nckm", cos_table) + product(
        arrived_im, "ncbk,bm->nckm", sin_table
    )
    spectrum_im = product(arrived_im, "ncbk,bm->nckm", cos_table) - product(
        arrived_re, "ncbk,bm->nckm", sin_table
    )
    return (spectrum_re, spectrum_im)


def inverse(spectrum_re, spectrum_im, deliver, restore, tables, location, length):
    cos_table, sin_table = tables
    factor = cos_table.shape[0]
    shrink = 1.0 / factor
    block_size = spectrum_re.shape[2]
    row_ids = location * block_size + jnp.arange(block_size, dtype=jnp.int32)
    wave_cos, wave_sin = twist_grid(row_ids, jnp.arange(factor, dtype=jnp.int32), length)
    unwound_re = (
        product(spectrum_re, "nckm,mb->nckb", cos_table)
        - product(spectrum_im, "nckm,mb->nckb", sin_table)
    ) * shrink
    unwound_im = (
        product(spectrum_im, "nckm,mb->nckb", cos_table)
        + product(spectrum_re, "nckm,mb->nckb", sin_table)
    ) * shrink
    untwisted = jnp.stack(
        [
            unwound_re * wave_cos - unwound_im * wave_sin,
            unwound_im * wave_cos + unwound_re * wave_sin,
        ],
        axis=1,
    ).astype(jnp.bfloat16)
    arrived = deliver(untwisted)
    values = (
        (
            product(arrived[:, 0], "nckb,ka->ncab", cos_table)
            - product(arrived[:, 1], "nckb,ka->ncab", sin_table)
        )
        * shrink
    ).astype(jnp.bfloat16)
    return restore(values)


def grouped(values, kernel):
    return values.reshape((-1,) + kernel.shape)


def forward_product(forward_re, forward_im, kernel_re, kernel_im):
    shape = forward_re.shape
    front_re = grouped(forward_re, kernel_re)
    front_im = grouped(forward_im, kernel_re)
    output_re = (front_re * kernel_re - front_im * kernel_im).astype(jnp.bfloat16).reshape(shape)
    output_im = (front_re * kernel_im + front_im * kernel_re).astype(jnp.bfloat16).reshape(shape)
    return (output_re, output_im)


def backward_product(backward_re, backward_im, kernel_re, kernel_im):
    shape = backward_re.shape
    back_re = grouped(backward_re, kernel_re)
    back_im = grouped(backward_im, kernel_re)
    input_re = (kernel_re * back_re + kernel_im * back_im).astype(jnp.bfloat16).reshape(shape)
    input_im = (kernel_re * back_im - kernel_im * back_re).astype(jnp.bfloat16).reshape(shape)
    return (input_re, input_im)


def per_device(outer_gate, inner_gate, signal, filter_spectrum, cotangent):
    channels, positions = signal.shape
    factor = filter_spectrum.shape[3]
    length = factor * factor
    row_count = positions // factor
    location = lax.axis_index("seq")
    tables = wave_tables(factor)
    mixed_input = (
        (inner_gate.astype(jnp.float32) * signal.astype(jnp.float32))
        .astype(jnp.bfloat16)
        .reshape(channels, row_count, factor)
    )
    gated_cotangent = (
        (cotangent.astype(jnp.float32) * outer_gate.astype(jnp.float32))
        .astype(jnp.bfloat16)
        .reshape(channels, row_count, factor)
    )
    kernel_re = filter_spectrum[0]
    kernel_im = filter_spectrum[1]

    def spread(stacked):
        return lax.all_to_all(stacked, "seq", split_axis=3, concat_axis=2, tiled=True)

    def collect(twisted):
        return lax.all_to_all(twisted, "seq", split_axis=4, concat_axis=3, tiled=True)

    def deliver(untwisted):
        return lax.all_to_all(untwisted, "seq", split_axis=4, concat_axis=3, tiled=True)

    def restore(values):
        return lax.all_to_all(values, "seq", split_axis=2, concat_axis=3, tiled=True)

    forward_re, forward_im = transform(mixed_input[None], spread, collect, tables, location, length)
    forward_re = forward_re[0]
    forward_im = forward_im[0]
    output_re, output_im = forward_product(forward_re, forward_im, kernel_re, kernel_im)
    long_output = inverse(
        output_re[None], output_im[None], deliver, restore, tables, location, length
    )[0]
    backward_re, backward_im = transform(
        gated_cotangent[None], spread, collect, tables, location, length
    )
    backward_re = backward_re[0]
    backward_im = backward_im[0]
    input_re, input_im = backward_product(backward_re, backward_im, kernel_re, kernel_im)
    mixed_gradient = inverse(
        input_re[None], input_im[None], deliver, restore, tables, location, length
    )[0]
    front_re = grouped(forward_re, kernel_re)
    front_im = grouped(forward_im, kernel_re)
    back_re = grouped(backward_re, kernel_re)
    back_im = grouped(backward_im, kernel_re)
    filter_re = jnp.sum(front_re * back_re + front_im * back_im, axis=0) / length
    filter_im = jnp.sum(front_re * back_im - front_im * back_re, axis=0) / length
    gradient_filter = lax.psum(
        jnp.stack([filter_re, filter_im]).astype(jnp.bfloat16), "chan"
    ).astype(jnp.float32)
    long_values = long_output.reshape(channels, positions).astype(jnp.float32)
    mixed_values = mixed_gradient.reshape(channels, positions).astype(jnp.float32)
    output = (outer_gate.astype(jnp.float32) * long_values).astype(jnp.bfloat16)
    gradient_outer = (cotangent.astype(jnp.float32) * long_values).astype(jnp.bfloat16)
    gradient_inner = (mixed_values * signal.astype(jnp.float32)).astype(jnp.bfloat16)
    gradient_signal = (mixed_values * inner_gate.astype(jnp.float32)).astype(jnp.bfloat16)
    return (output, gradient_outer, gradient_inner, gradient_signal, gradient_filter)


def solution(mesh):
    in_specs = (
        P("chan", "seq"),
        P("chan", "seq"),
        P("chan", "seq"),
        P(None, None, "seq", None),
        P("chan", "seq"),
    )
    out_specs = (
        P("chan", "seq"),
        P("chan", "seq"),
        P("chan", "seq"),
        P("chan", "seq"),
        P(None, None, "seq", None),
    )
    return jax.shard_map(
        per_device, mesh=mesh, in_specs=in_specs, out_specs=out_specs, check_vma=False
    )
```

profile of v0, /device:TPU:0, one launch (start us, length us, event | category | flops | bytes accessed | tf_op | source)
XLA Modules:
  0.0 1700.4 jit_solution(7797973607591189532)
XLA Ops:
  77.6 61.7 %all-to-all-done.4 = bf16[8,2,131072]{2,1,0:T(2,128)(2,1)} async-done(((bf16[8,2,131072]{2,1,0:T(2,128)(2,1)}), bf16[8,2,131072]{2,1,0:T(2,128)(2,1)}, u32[]{:S(2)}, u32[]{:S(2)}) %all-to-all-start.4) | async-done | bytes 4194336 | tf_op jit(solution)/shard_map/all_to_all | solution.py:130
  211.1 25.5 %all-to-all-done = bf16[8,2,131072]{2,1,0:T(2,128)(2,1)} async-done(((bf16[8,2,131072]{2,1,0:T(2,128)(2,1)}), bf16[8,2,131072]{2,1,0:T(2,128)(2,1)}, u32[]{:S(2)}, u32[]{:S(2)}) %all-to-all-start) | async-done | bytes 4194336 | tf_op jit(solution)/shard_map/all_to_all | solution.py:130
  314.9 24.0 %copy.43 = bf16[1,2,64,64,512]{3,2,1,0,4:T(8,128)(2,1)} copy(bf16[1,2,64,64,512]{4,3,2,1,0:T(8,128)(2,1)} %get-tuple-element.41) | data formatting | bytes 16777216 | tf_op jit(solution)/shard_map/stack | solution.py:35
  338.9 16.9 reshape.445
  360.7 24.0 %copy.52 = bf16[1,2,64,64,512]{3,2,1,0,4:T(8,128)(2,1)} copy(bf16[1,2,64,64,512]{4,3,2,1,0:T(8,128)(2,1)} %get-tuple-element.42) | data formatting | bytes 16777216 | tf_op jit(solution)/shard_map/stack | solution.py:35
  384.7 16.9 reshape.453
  401.6 141.1 %all-to-all-done.1 = bf16[8,2,262144]{2,1,0:T(2,128)(2,1)} async-done(((bf16[8,2,262144]{2,1,0:T(2,128)(2,1)}), bf16[8,2,262144]{2,1,0:T(2,128)(2,1)}, u32[]{:S(2)}, u32[]{:S(2)}) %all-to-all-start.1) | async-done | bytes 8388640 | tf_op jit(solution)/shard_map/all_to_all | solution.py:133
  549.0 16.5 reshape.446
  565.4 18.7 %copy.69 = bf16[1,2,64,64,8,64]{3,4,5,2,1,0:T(8,128)(2,1)} copy(bf16[1,2,64,64,8,64]{3,2,1,5,4,0:T(8,128)(2,1)} %bitcast.264) | data formatting | bytes 16777216 | tf_op jit(solution)/shard_map/all_to_all | solution.py:133
  584.1 22.5 %all_to_all.94 = bf16[1,2,64,512,64]{3,4,2,1,0:T(8,128)(2,1)} reshape(bf16[1,2,64,8,64,64]{4,3,5,2,1,0:T(8,128)(2,1)} %bitcast.265) | data formatting | bytes 16777216 | tf_op jit(solution)/shard_map/all_to_all | solution.py:133
  625.8 104.2 %all-to-all-done.5 = bf16[8,2,262144]{2,1,0:T(2,128)(2,1)} async-done(((bf16[8,2,262144]{2,1,0:T(2,128)(2,1)}), bf16[8,2,262144]{2,1,0:T(2,128)(2,1)}, u32[]{:S(2)}, u32[]{:S(2)}) %all-to-all-start.5) | async-done | bytes 8388640 | tf_op jit(solution)/shard_map/all_to_all | solution.py:133
  730.0 16.5 reshape.454
  746.4 18.9 %copy.67 = bf16[1,2,64,64,8,64]{3,4,5,2,1,0:T(8,128)(2,1)} copy(bf16[1,2,64,64,8,64]{3,2,1,5,4,0:T(8,128)(2,1)} %bitcast.266) | data formatting | bytes 16777216 | tf_op jit(solution)/shard_map/all_to_all | solution.py:133
  765.4 22.5 %all_to_all.106 = bf16[1,2,64,512,64]{3,4,2,1,0:T(8,128)(2,1)} reshape(bf16[1,2,64,8,64,64]{4,3,5,2,1,0:T(8,128)(2,1)} %bitcast.267) | data formatting | bytes 16777216 | tf_op jit(solution)/shard_map/all_to_all | solution.py:133
  833.8 23.7 %multiply_add_fusion = (f32[64,64,512]{2,1,0:T(8,128)}, f32[64,64,512]{2,1,0:T(8,128)}, bf16[64,64,512]{2,1,0:T(8,128)(2,1)}, bf16[64,64,512]{2,1,0:T(8,128)(2,1...) fusion(f32[64,64,512]{2,1,0:T(8,128)} %fusion.33, f32[64,64,512]{2,1,0:T(8,128)} %fusion.34, ...), kind=kOutput, calls=%fused_computation.39 | convolution fusion | flops 2199650304 | bytes 72351744 | tf_op jit(solution)/shard_map/ncbk,bm->nckm/dot_general | solution.py:23
  919.2 27.1 %fusion.21 = (bf16[1,1,64,64,512]{4,3,2,1,0:T(8,128)(2,1)}, bf16[1,1,64,64,512]{4,3,2,1,0:T(8,128)(2,1)}, bf16[1,1,64,64,512]{4,3,2,1,0:T(8,128)(2,1)}, bf16[1,1,64,64,512]{4,3,2,1,0:T(8,128)(2,1)}) fusion(f32[64,512]{1,0:T(8,128)S(1)} %copy-done.8, f32[64,512]{1,0:T(8,128)S(1)} %copy-done.9, f32[64,64,512]{2,1,0:T(8,128)} %fusion.58, ...), kind=kOutput, calls=%fused_computation.57 | convolution fusion | flops 2193358848 | bytes 79953920 | tf_op jit(solution)/shard_map/nckm,mb->nckb/dot_general | solution.py:23
  953.9 24.0 %copy.54 = bf16[1,2,64,64,512]{3,2,1,0,4:T(8,128)(2,1)} copy(bf16[1,2,64,64,512]{4,3,2,1,0:T(8,128)(2,1)} %pad_maximum_fusion.3) | data formatting | bytes 16777216 | tf_op jit(solution)/shard_map/stack | solution.py:69
  977.9 17.0 %reshape.455 = bf16[8,2,262144]{2,1,0:T(2,128)(2,1)} reshape(bf16[512,1,2,64,64]{4,3,2,1,0:T(8,128)(2,1)} %bitcast.262) | data formatting | bytes 16777216
  1007.3 24.0 %copy.45 = bf16[1,2,64,64,512]{3,2,1,0,4:T(8,128)(2,1)} copy(bf16[1,2,64,64,512]{4,3,2,1,0:T(8,128)(2,1)} %pad_maximum_fusion.1) | data formatting | bytes 16777216 | tf_op jit(solution)/shard_map/stack | solution.py:69
  1031.3 16.8 reshape.447
  1048.1 133.9 %all-to-all-done.6 = bf16[8,2,262144]{2,1,0:T(2,128)(2,1)} async-done(((bf16[8,2,262144]{2,1,0:T(2,128)(2,1)}), bf16[8,2,262144]{2,1,0:T(2,128)(2,1)}, u32[]{:S(2)}, u32[]{:S(2)}) %all-to-all-start.6) | async-done | bytes 8388640 | tf_op jit(solution)/shard_map/all_to_all | solution.py:136
  1187.0 16.5 reshape.456
  1203.5 18.7 %copy.66 = bf16[1,2,64,64,8,64]{3,4,5,2,1,0:T(8,128)(2,1)} copy(bf16[1,2,64,64,8,64]{3,2,1,5,4,0:T(8,128)(2,1)} %bitcast.268) | data formatting | bytes 16777216 | tf_op jit(solution)/shard_map/all_to_all | solution.py:136
  1222.2 22.5 %all_to_all.110 = bf16[1,2,64,512,64]{3,4,2,1,0:T(8,128)(2,1)} reshape(bf16[1,2,64,8,64,64]{4,3,5,2,1,0:T(8,128)(2,1)} %bitcast.269) | data formatting | bytes 16777216 | tf_op jit(solution)/shard_map/all_to_all | solution.py:136
  1299.1 70.1 %all-to-all-done.2 = bf16[8,2,262144]{2,1,0:T(2,128)(2,1)} async-done(((bf16[8,2,262144]{2,1,0:T(2,128)(2,1)}), bf16[8,2,262144]{2,1,0:T(2,128)(2,1)}, u32[]{:S(2)}, u32[]{:S(2)}) %all-to-all-start.2) | async-done | bytes 8388640 | tf_op jit(solution)/shard_map/all_to_all | solution.py:136
  1383.6 34.8 %all-reduce.2.cloned.1.call-done = bf16[2,4,64,512]{3,2,1,0:T(8,128)(2,1)} async-done(((bf16[2,4,64,512]{3,2,1,0:T(8,128)(2,1)}), bf16[2,4,64,512]{3,2,1,0:T(8,128)(2,1)}) %all-reduce.2.cloned.1.call-update) | async-done | bytes 524304 | tf_op jit(solution)/shard_map/psum | solution.py:163
  1420.5 16.9 reshape.448
  1437.4 18.7 %copy.68 = bf16[1,2,64,64,8,64]{3,4,5,2,1,0:T(8,128)(2,1)} copy(bf16[1,2,64,64,8,64]{3,2,1,5,4,0:T(8,128)(2,1)} %bitcast.270) | data formatting | bytes 16777216 | tf_op jit(solution)/shard_map/all_to_all | solution.py:136
  1456.1 22.5 %all_to_all.98 = bf16[1,2,64,512,64]{3,4,2,1,0:T(8,128)(2,1)} reshape(bf16[1,2,64,8,64,64]{4,3,5,2,1,0:T(8,128)(2,1)} %bitcast.271) | data formatting | bytes 16777216 | tf_op jit(solution)/shard_map/all_to_all | solution.py:136
  1560.1 17.8 %copy.57 = f32[1,64,64,8,64]{4,3,2,1,0:T(8,128)} copy(f32[1,64,64,8,64]{4,1,2,3,0:T(8,128)} %convert_bitcast_fusion) | data formatting | bytes 16777216 | tf_op jit(solution)/shard_map/convert_element_type | solution.py:167
  1600.9 29.6 %all-to-all-done.3 = bf16[8,2,131072]{2,1,0:T(2,128)(2,1)} async-done(((bf16[8,2,131072]{2,1,0:T(2,128)(2,1)}), bf16[8,2,131072]{2,1,0:T(2,128)(2,1)}, u32[]{:S(2)}, u32[]{:S(2)}) %all-to-all-start.3) | async-done | bytes 4194336 | tf_op jit(solution)/shard_map/all_to_all | solution.py:139
  1652.3 18.0 %copy.48 = f32[1,64,64,8,64]{4,3,2,1,0:T(8,128)} copy(f32[1,64,64,8,64]{4,1,2,3,0:T(8,128)} %convert_bitcast_fusion.1) | data formatting | bytes 16777216 | tf_op jit(solution)/shard_map/convert_element_type | solution.py:166
  (102 shorter events, 603.6 us)
Async XLA Ops:
  38.7 100.6 %all-to-all-start.4 = ((bf16[8,2,131072]{2,1,0:T(2,128)(2,1)}), bf16[8,2,131072]{2,1,0:T(2,128)(2,1)}, u32[]{:S(2)}, u32[]{:S(2)}) async-start(bf16[8,2,131072]{2,1,0:T(2,128)(2,1)} %reshape.451), calls=%async_computation.4 | async-start | bytes 8388608 | tf_op jit(solution)/shard_map/all_to_all | solution.py:130
  139.3 97.3 %all-to-all-start = ((bf16[8,2,131072]{2,1,0:T(2,128)(2,1)}), bf16[8,2,131072]{2,1,0:T(2,128)(2,1)}, u32[]{:S(2)}, u32[]{:S(2)}) async-start(bf16[8,2,131072]{2,1,0:T(2,128)(2,1)} %reshape.443), calls=%async_computation | async-start | bytes 8388608 | tf_op jit(solution)/shard_map/all_to_all | solution.py:130
  192.1 10.8 copy-start.6
  283.7 10.8 copy-start.2
  355.8 187.0 %all-to-all-start.1 = ((bf16[8,2,262144]{2,1,0:T(2,128)(2,1)}), bf16[8,2,262144]{2,1,0:T(2,128)(2,1)}, u32[]{:S(2)}, u32[]{:S(2)}) async-start(bf16[8,2,262144]{2,1,0:T(2,128)(2,1)} %reshape.445), calls=%async_computation.1 | async-start | bytes 16777216 | tf_op jit(solution)/shard_map/all_to_all | solution.py:133
  401.6 146.3 %copy-start.7 = (f32[2,4,64,512]{3,2,1,0:T(8,128)S(1)}, f32[2,4,64,512]{3,2,1,0:T(8,128)}, u32[]{:S(2)}) copy-start(f32[2,4,64,512]{3,2,1,0:T(8,128)} %param.8) | copy-start | bytes 3145732
  542.7 187.2 %all-to-all-start.5 = ((bf16[8,2,262144]{2,1,0:T(2,128)(2,1)}), bf16[8,2,262144]{2,1,0:T(2,128)(2,1)}, u32[]{:S(2)}, u32[]{:S(2)}) async-start(bf16[8,2,262144]{2,1,0:T(2,128)(2,1)} %reshape.453), calls=%async_computation.5 | async-start | bytes 16777216 | tf_op jit(solution)/shard_map/all_to_all | solution.py:133
  606.6 10.8 copy-start
  787.8 10.6 copy-start.1
  787.8 15.9 slice-start
  798.5 5.2 slice-start.1
  857.5 10.8 copy-start.5
  868.3 8.4 copy-start.4
  885.2 8.4 copy-start.3
  910.8 8.4 copy-start.8
  910.8 8.4 copy-start.9
  994.9 187.2 %all-to-all-start.6 = ((bf16[8,2,262144]{2,1,0:T(2,128)(2,1)}), bf16[8,2,262144]{2,1,0:T(2,128)(2,1)}, u32[]{:S(2)}, u32[]{:S(2)}) async-start(bf16[8,2,262144]{2,1,0:T(2,128)(2,1)} %reshape.455), calls=%async_computation.6 | async-start | bytes 16777216 | tf_op jit(solution)/shard_map/all_to_all | solution.py:136
  1182.0 187.2 %all-to-all-start.2 = ((bf16[8,2,262144]{2,1,0:T(2,128)(2,1)}), bf16[8,2,262144]{2,1,0:T(2,128)(2,1)}, u32[]{:S(2)}, u32[]{:S(2)}) async-start(bf16[8,2,262144]{2,1,0:T(2,128)(2,1)} %reshape.447), calls=%async_computation.2 | async-start | bytes 16777216 | tf_op jit(solution)/shard_map/all_to_all | solution.py:136
  1369.2 163.7 %all-to-all-start.7 = ((bf16[8,2,131072]{2,1,0:T(2,128)(2,1)}), bf16[8,2,131072]{2,1,0:T(2,128)(2,1)}, u32[]{:S(2)}, u32[]{:S(2)}) async-start(bf16[8,2,131072]{2,1,0:T(2,128)(2,1)} %reshape.457), calls=%async_computation.7 | async-start | bytes 8388608 | tf_op jit(solution)/shard_map/all_to_all | solution.py:139
  1373.8 44.6 %all-reduce.2.cloned.1.call-start = ((), (), s32[]{:S(2)}) async-start(), calls=%async_computation.8 | async-start | bytes 1048576 | tf_op jit(solution)/shard_map/psum | solution.py:163
  1532.9 97.7 %all-to-all-start.3 = ((bf16[8,2,131072]{2,1,0:T(2,128)(2,1)}), bf16[8,2,131072]{2,1,0:T(2,128)(2,1)}, u32[]{:S(2)}, u32[]{:S(2)}) async-start(bf16[8,2,131072]{2,1,0:T(2,128)(2,1)} %reshape.449), calls=%async_computation.3 | async-start | bytes 8388608 | tf_op jit(solution)/shard_map/all_to_all | solution.py:139
Sparse Core Ops, SparseCore 0:
  1383.7 34.6 all-reduce.1
where the time goes:
time: 1720 us; the launch traced here: 1700 us
  local copies, waits for them, and re-layouts  681 us (40%)
  waiting for transfers between devices  601 us (35%)
  matrix products  256 us (15%)
  other arithmetic  106 us (6%)
  starting transfers between devices  42.2 us (2%)
    all_to_all x2, waiting for transfers between devices, collect(): lax.all_to_all(twisted, 'seq', split_axis=4, concat_axis=3, tiled=True)  245 us
    unnamed x42, local copies, waits for them, and re-layouts  225 us
    dot_general x20, matrix products, product(): jnp.einsum(pattern, operand, matrix, preferred_element_type=jnp.float32)  222 us
    all_to_all x2, waiting for transfers between devices, deliver(): lax.all_to_all(untwisted, 'seq', split_axis=4, concat_axis=3, tiled=True)  204 us
    all_to_all x2, waiting for transfers between devices, spread(): lax.all_to_all(stacked, 'seq', split_axis=3, concat_axis=2, tiled=True)  87.2 us
    all_to_all x4, local copies, waits for them, and re-layouts, collect(): lax.all_to_all(twisted, 'seq', split_axis=4, concat_axis=3, tiled=True)  82.5 us
    all_to_all x4, local copies, waits for them, and re-layouts, deliver(): lax.all_to_all(untwisted, 'seq', split_axis=4, concat_axis=3, tiled=True)  82.3 us
    all_to_all x4, local copies, waits for them, and re-layouts, spread(): lax.all_to_all(stacked, 'seq', split_axis=3, concat_axis=2, tiled=True)  49.3 us
  transfers between devices with their start and end apart: 9, of which 8 were waited for; matrix products, arithmetic and copies ran while one was open for 29% of the time, Pallas kernels for 0%

commit v1 on v0

--- a/solution.py
+++ b/solution.py
@@ -1,9 +1,15 @@
+import functools
 import math
 
 import jax
 import jax.numpy as jnp
 from jax import lax
+from jax.experimental import pallas as pl
+from jax.experimental.pallas import tpu as pltpu
 from jax.sharding import PartitionSpec as P
+
+MESH = pl.DeviceIdType.MESH
+VMEM_BYTES = 56 * 1024 * 1024
 
 
 def wave_tables(factor):
@@ -172,6 +178,297 @@
     return (output, gradient_outer, gradient_inner, gradient_signal, gradient_filter)
 
 
+def channel_slots(channels, filters, devices):
+    if channels % devices or devices % filters:
+        return 0
+    return devices // filters
+
+
+def pack_kernel(filters, rows, outer_ref, inner_ref, signal_ref, cotangent_ref, send_ref):
+    factor = send_ref.shape[-1]
+    products = (
+        inner_ref[...].astype(jnp.float32) * signal_ref[...].astype(jnp.float32),
+        cotangent_ref[...].astype(jnp.float32) * outer_ref[...].astype(jnp.float32),
+    )
+    for which, values in enumerate(products):
+        pieces = jnp.stack([values[:, factor * r : factor * (r + 1)] for r in range(rows)], axis=0)
+        turned = jnp.transpose(pieces, (1, 0, 2)).astype(jnp.bfloat16)
+        for c in range(turned.shape[0]):
+            send_ref[c % filters, 0, c // filters, which] = turned[c]
+
+
+def unpack_kernel(
+    filters, rows, back_ref, outer_ref, inner_ref, signal_ref, cotangent_ref, out_ref, d_outer, d_inner, d_signal
+):
+    factor = back_ref.shape[-1]
+    count = outer_ref.shape[0]
+    targets = (((out_ref, outer_ref), (d_outer, cotangent_ref)), ((d_inner, signal_ref), (d_signal, inner_ref)))
+    for which, pairs in enumerate(targets):
+        turned = jnp.stack(
+            [back_ref[c % filters, 0, c // filters, which].astype(jnp.float32) for c in range(count)], axis=0
+        )
+        pieces = jnp.transpose(turned, (1, 0, 2))
+        for r in range(rows):
+            columns = slice(factor * r, factor * (r + 1))
+            for target, gate in pairs:
+                target[:, columns] = (gate[:, columns].astype(jnp.float32) * pieces[r]).astype(jnp.bfloat16)
+
+
+def convolve_kernel(
+    devices,
+    shares,
+    send_ref,
+    taps_ref,
+    cs_ref,
+    ahead_ref,
+    behind_ref,
+    last_ref,
+    wave_cos_ref,
+    wave_sin_ref,
+    back_ref,
+    grads_ref,
+    held,
+    made,
+    taps,
+    grads,
+    grads_sent,
+    straight,
+    filtered,
+    unwound,
+    send_sems,
+    recv_sems,
+    back_send_sems,
+    back_recv_sems,
+    small_send_sems,
+    small_recv_sems,
+):
+    me = lax.axis_index("seq")
+    count, rows, factor = send_ref.shape[1], send_ref.shape[3], send_ref.shape[4]
+    step = held.shape[0] // 2 * rows
+    length = factor * factor
+
+    def peer(offset):
+        return lax.rem(me + offset, devices)
+
+    def copy(source, target, offset, send_sem, recv_sem):
+        return pltpu.make_async_remote_copy(
+            src_ref=source,
+            dst_ref=target,
+            send_sem=send_sem,
+            recv_sem=recv_sem,
+            device_id={"seq": peer(offset)},
+            device_id_type=MESH,
+        )
+
+    def own(source, target, sem):
+        return pltpu.make_async_copy(source, target, sem)
+
+    def forth(offset, c):
+        source = send_ref.at[peer(offset), c]
+        if offset == 0:
+            return own(source, held.at[me, c], recv_sems.at[0, c])
+        return copy(source, held.at[me, c], offset, send_sems.at[offset, c], recv_sems.at[offset, c])
+
+    def back(offset, c):
+        source = made.at[c, peer(offset)]
+        if offset == 0:
+            return own(source, back_ref.at[me, c], back_recv_sems.at[0, c])
+        return copy(source, back_ref.at[me, c], offset, back_send_sems.at[offset, c], back_recv_sems.at[offset, c])
+
+    def tap(offset):
+        source = taps_ref.at[peer(offset) // shares]
+        if offset == 0:
+            return own(source, taps.at[me], small_recv_sems.at[0, 0])
+        return copy(source, taps.at[me], offset, small_send_sems.at[0, offset], small_recv_sems.at[0, offset])
+
+    def grad(offset):
+        source = grads_sent.at[peer(offset)]
+        if offset == 0:
+            return own(source, grads_ref.at[me], small_recv_sems.at[1, 0])
+        return copy(source, grads_ref.at[me], offset, small_send_sems.at[1, offset], small_recv_sems.at[1, offset])
+
+    order = [0] + [k for pair in zip(range(1, devices), range(devices - 1, 0, -1)) for k in pair][: devices - 1]
+
+    barrier = pltpu.get_barrier_semaphore()
+    for offset in range(1, devices):
+        pl.semaphore_signal(barrier, inc=1, device_id={"seq": peer(offset)}, device_id_type=MESH)
+    pl.semaphore_wait(barrier, devices - 1)
+
+    for offset in order:
+        tap(offset).start()
+
+    @pl.loop(0, count)
+    def _(c):
+        for offset in order:
+            forth(offset, c).start()
+
+    grads[...] = jnp.zeros_like(grads)
+    for offset in order:
+        if offset == 0:
+            tap(offset).wait()
+        else:
+            tap(offset).wait_recv()
+
+    def dot(left, right):
+        return jnp.dot(left, right, preferred_element_type=jnp.float32)
+
+    @pl.loop(0, count)
+    def _(c):
+        for offset in order:
+            if offset == 0:
+                forth(offset, c).wait()
+            else:
+                forth(offset, c).wait_recv()
+
+        @pl.loop(0, 2)
+        def _(half):
+            span = pl.ds(pl.multiple_of(half * step, step), step)
+            low = pl.ds(pl.multiple_of(factor + half * step, step), step)
+            wave_cos = wave_cos_ref[span, :]
+            wave_sin = wave_sin_ref[span, :]
+            spectra = []
+            for which in range(2):
+                source = held[:, c, which].reshape(factor, factor)
+                p = dot(cs_ref[span, :], source)
+                q = dot(cs_ref[low, :], source)
+                straight[which, :, :factor] = (p * wave_cos - q * wave_sin).astype(jnp.bfloat16)
+                straight[which, :, factor:] = (-q * wave_cos - p * wave_sin).astype(jnp.bfloat16)
+            for which in range(2):
+                spectrum = dot(straight[which], ahead_ref[...])
+                spectra.append((spectrum[:, :factor], spectrum[:, factor:]))
+            quarter = held.shape[0] // 2
+            blocks = pl.ds(half * quarter, quarter)
+            tap_re = taps[blocks, 0].reshape(step, factor).astype(jnp.float32)
+            tap_im = taps[blocks, 1].reshape(step, factor).astype(jnp.float32)
+            (f_re, f_im), (b_re, b_im) = spectra
+            grads[0, span, :] += f_re * b_re + f_im * b_im
+            grads[1, span, :] += f_re * b_im - f_im * b_re
+            filtered[0, :, :factor] = (f_re * tap_re - f_im * tap_im).astype(jnp.bfloat16)
+            filtered[0, :, factor:] = (f_re * tap_im + f_im * tap_re).astype(jnp.bfloat16)
+            filtered[1, :, :factor] = (tap_re * b_re + tap_im * b_im).astype(jnp.bfloat16)
+            filtered[1, :, factor:] = (tap_re * b_im - tap_im * b_re).astype(jnp.bfloat16)
+            for which in range(2):
+                values = dot(filtered[which], behind_ref[...])
+                u_re, u_im = values[:, :factor], values[:, factor:]
+                unwound[which, span, :] = (u_re * wave_cos - u_im * wave_sin).astype(jnp.bfloat16)
+                unwound[which, low, :] = (u_im * wave_cos + u_re * wave_sin).astype(jnp.bfloat16)
+
+        for which in range(2):
+            values = (dot(last_ref[...], unwound[which]) * (1.0 / length)).astype(jnp.bfloat16)
+            made[c, :, which] = values.reshape(devices, rows, factor)
+        for offset in order:
+            back(offset, c).start()
+
+    for part in range(2):
+        scaled = (grads[part] * (1.0 / length)).astype(jnp.bfloat16)
+        grads_sent[:, part] = scaled.reshape(devices, rows, factor)
+    for offset in order:
+        grad(offset).start()
+    for offset in order:
+        if offset == 0:
+            grad(offset).wait()
+        else:
+            grad(offset).wait()
+            tap(offset).wait_send()
+
+    @pl.loop(0, count)
+    def _(c):
+        for offset in order:
+            if offset == 0:
+                back(offset, c).wait()
+            else:
+                forth(offset, c).wait_send()
+                back(offset, c).wait()
+
+
+def by_channels(devices, shares, outer_gate, inner_gate, signal, filter_spectrum, cotangent):
+    channels, positions = signal.shape
+    filters, factor = filter_spectrum.shape[1], filter_spectrum.shape[3]
+    rows = positions // factor
+    count = channels // devices
+    length = factor * factor
+    block, depth = 16, 16
+    per = block // filters
+    split = count // per
+    line = pl.BlockSpec((block, depth * factor), lambda i, t: (i, t))
+    boxes = pl.BlockSpec(
+        (filters, 1, per, 2, depth, factor), lambda i, t: (0, i // split, i % split, 0, t, 0)
+    )
+    grid = (channels // block, rows // depth)
+    box_shape = (filters, shares, count, 2, rows, factor)
+    limit = pltpu.CompilerParams(vmem_limit_bytes=VMEM_BYTES)
+    send = pl.pallas_call(
+        functools.partial(pack_kernel, filters, depth),
+        grid=grid,
+        in_specs=[line] * 4,
+        out_specs=boxes,
+        out_shape=jax.ShapeDtypeStruct(box_shape, jnp.bfloat16),
+        compiler_params=limit,
+        name="pack",
+    )(outer_gate, inner_gate, signal, cotangent)
+    send = send.reshape(devices, count, 2, rows, factor)
+    cos_table, sin_table = wave_tables(factor)
+    ordinal = jnp.arange(factor, dtype=jnp.int32)
+    wave_cos, wave_sin = twist_grid(ordinal, ordinal, length)
+    cs = jnp.concatenate([cos_table, sin_table], axis=0)
+    ahead = jnp.block([[cos_table, -sin_table], [sin_table, cos_table]])
+    behind = jnp.block([[cos_table, sin_table], [-sin_table, cos_table]])
+    last = jnp.concatenate([cos_table, -sin_table], axis=1)
+    taps = filter_spectrum.astype(jnp.bfloat16).transpose(1, 0, 2, 3)
+    anywhere = pl.BlockSpec(memory_space=pl.ANY)
+    inside = pl.BlockSpec(memory_space=pltpu.VMEM)
+    back, grads = pl.pallas_call(
+        functools.partial(convolve_kernel, devices, shares),
+        in_specs=[anywhere, anywhere] + [inside] * 6,
+        out_specs=[anywhere, anywhere],
+        out_shape=[
+            jax.ShapeDtypeStruct((devices, count, 2, rows, factor), jnp.bfloat16),
+            jax.ShapeDtypeStruct((devices, 2, rows, factor), jnp.bfloat16),
+        ],
+        scratch_shapes=[
+            pltpu.VMEM((devices, count, 2, rows, factor), jnp.bfloat16),
+            pltpu.VMEM((count, devices, 2, rows, factor), jnp.bfloat16),
+            pltpu.VMEM((devices, 2, rows, factor), jnp.bfloat16),
+            pltpu.VMEM((2, factor, factor), jnp.float32),
+            pltpu.VMEM((devices, 2, rows, factor), jnp.bfloat16),
+            pltpu.VMEM((2, factor // 2, 2 * factor), jnp.bfloat16),
+            pltpu.VMEM((2, factor // 2, 2 * factor), jnp.bfloat16),
+            pltpu.VMEM((2, 2 * factor, factor), jnp.bfloat16),
+            pltpu.SemaphoreType.DMA((devices, count)),
+            pltpu.SemaphoreType.DMA((devices, count)),
+            pltpu.SemaphoreType.DMA((devices, count)),
+            pltpu.SemaphoreType.DMA((devices, count)),
+            pltpu.SemaphoreType.DMA((2, devices)),
+            pltpu.SemaphoreType.DMA((2, devices)),
+        ],
+        compiler_params=pltpu.CompilerParams(
+            collective_id=0, has_side_effects=True, vmem_limit_bytes=VMEM_BYTES
+        ),
+        name="convolve",
+    )(send, taps, cs, ahead, behind, last, wave_cos, wave_sin)
+    shared = grads.astype(jnp.float32).reshape(filters, shares, 2, rows, factor).sum(axis=1)
+    gradient_filter = lax.psum(
+        shared.transpose(1, 0, 2, 3).astype(jnp.bfloat16), "chan"
+    ).astype(jnp.float32)
+    outputs = pl.pallas_call(
+        functools.partial(unpack_kernel, filters, depth),
+        grid=grid,
+        in_specs=[boxes] + [line] * 4,
+        out_specs=[line] * 4,
+        out_shape=[jax.ShapeDtypeStruct((channels, positions), jnp.bfloat16)] * 4,
+        compiler_params=limit,
+        name="unpack",
+    )(back.reshape(box_shape), outer_gate, inner_gate, signal, cotangent)
+    return (*outputs, gradient_filter)
+
+
+def local_program(devices, outer_gate, inner_gate, signal, filter_spectrum, cotangent):
+    filters = filter_spectrum.shape[1]
+    shares = channel_slots(signal.shape[0], filters, devices)
+    program = functools.partial(by_channels, devices, shares) if shares else per_device
+    return program(outer_gate, inner_gate, signal, filter_spectrum, cotangent)
+
+
 def solution(mesh):
     in_specs = (
         P("chan", "seq"),
@@ -188,5 +485,5 @@
         P(None, None, "seq", None),
     )
     return jax.shard_map(
-        per_device, mesh=mesh, in_specs=in_specs, out_specs=out_specs, check_vma=False
-    )
+        functools.partial(local_program, mesh.shape["seq"]), mesh=mesh, in_specs=in_specs, out_specs=out_specs, check_vma=False
+    )

time: 1720 us -> 512 us (0.30); the launches traced: 1700 us -> 511 us
  local copies, waits for them, and re-layouts: 681 us -> 3.01 us
  waiting for transfers between devices: 601 us -> 13 us
  Pallas kernels: 0 us -> 453 us
  matrix products: 256 us -> 0 us
  other arithmetic: 106 us -> 27.7 us
  starting transfers between devices: 42.2 us -> 0.04 us
    all_to_all x8 -> x0, waiting for transfers between devices: 566 us -> none  [the longest x2 245 us: collect(): lax.all_to_all(twisted, 'seq', split_axis=4, concat_axis=3, tiled=True)]
    pallas_call x0 -> x3, Pallas kernels: none -> 453 us  [the longest x1 418 us: by_channels(): pl.pallas_call(functools.partial(convolve_kernel, devices, shares), in_sp...]
    unnamed x42 -> x4, local copies, waits for them, and re-layouts: 225 us -> 3.01 us
    dot_general x20 -> x0, matrix products: 222 us -> none  [product(): jnp.einsum(pattern, operand, matrix, preferred_element_type=jnp.float32)]
    all_to_all x12 -> x0, local copies, waits for them, and re-layouts: 214 us -> none  [the longest x4 82.5 us: collect(): lax.all_to_all(twisted, 'seq', split_axis=4, concat_axis=3, tiled=True)]
    another operation x7 -> x0, local copies, waits for them, and re-layouts: 134 us -> none  [the longest x2 47.9 us: transform(): jnp.stack([sectioned_re * wave_cos + sectioned_im * wave_sin, sectioned_i...]
    convert_element_type x6 -> x0, local copies, waits for them, and re-layouts: 87.7 us -> none  [the longest x2 31 us: per_device(): long_values = long_output.reshape(channels, positions).astype(jnp.float32)]
    convert_element_type x9 -> x1, other arithmetic: 74 us -> 4.31 us  [wave_tables(): jnp.sin(angles).astype(jnp.bfloat16)]
  transfers between devices with their start and end apart: 9 -> 1, of which waited for: 8 -> 1; matrix products, arithmetic and copies ran while one was open for 29% -> 0% of each run, Pallas kernels for 0% -> 4%
where the time goes in v1:
time: 512 us; the launch traced here: 511 us
  Pallas kernels  453 us (88%)
  other arithmetic  27.7 us (5%)
  between operations  14.1 us (3%)
  waiting for transfers between devices  13 us (3%)
    pallas_call x1, Pallas kernels, by_channels(): pl.pallas_call(functools.partial(convolve_kernel, devices, shares), in_sp...  418 us
    pallas_call x1, Pallas kernels, by_channels(): pl.pallas_call(functools.partial(unpack_kernel, filters, depth), grid=gri...  19.6 us
    pallas_call x1, Pallas kernels, by_channels(): pl.pallas_call(functools.partial(pack_kernel, filters, depth), grid=grid,...  15.4 us
    psum x1, waiting for transfers between devices, by_channels(): lax.psum(shared.transpose(1, 0, 2, 3).astype(jnp.bfloat16), 'chan')  12.9 us
  transfers between devices with their start and end apart: 1, of which 1 were waited for; matrix products, arithmetic and copies ran while one was open for 0% of the time, Pallas kernels for 4%

profile of v1, /device:TPU:0, one launch (start us, length us, event | category | flops | bytes accessed | tf_op | source)
XLA Modules:
  0.0 511.0 jit_solution(5237227040423043663)
XLA Ops:
  7.2 0.0 all-reduce.2.cloned.1.call-start
  7.2 4.0 fusion.16
  11.2 4.3 sine_convert_fusion
  15.5 4.9 fusion.14
  20.5 1.0 pad_maximum_fusion.4.cs_ref
  21.5 0.0 copy-start
  21.5 1.1 pad_maximum_fusion.5.last_ref
  22.6 10.0 %fusion.1 = (bf16[1024,1024]{1,0:T(8,128)(2,1)}, bf16[1024,1024]{1,0:T(8,128)(2,1)}) fusion(bf16[512,512]{1,0:T(8,128)(2,1)S(1)} %get-tuple-element.25, bf16[512,512]{1,0:T(8,128)(2,1)S(1)} %fusion.16, bf16[512,512]{1,0:T(8,128)(2,1)S(1)} %get-tuple-element.24), kind=kLoop, calls=%fused_computation.5 | loop fusion | flops 14680064 | bytes 5767168 | tf_op jit(solution)/shard_map/jit(block)/concatenate | solution.py:415
  32.6 0.0 copy-done
  32.6 0.9 copy.16
  33.4 15.4 %pack.1 = bf16[4,2,8,2,64,512]{5,4,3,2,1,0:T(8,128)(2,1)} custom-call(bf16[64,32768]{1,0:T(8,128)(2,1)} %outer_ref.3, bf16[64,32768]{1,0:T(8,128)(2,1)} %inner_ref.3, bf16[64,32768]{1,0:T(8,128)(2,1)} %signal_ref.3, bf16[64,32768]{1,0:T(8,128)(2,1)} %cotangent_ref.3), custom_call_target="tpu_custom_call" | custom-call | tf_op jit(solution)/shard_map/pack/pallas_call | solution.py:400
  48.8 418.2 %convolve.1 = (bf16[8,8,2,64,512]{4,3,2,1,0:T(8,128)(2,1)}, bf16[8,2,64,512]{3,2,1,0:T(8,128)(2,1)}) custom-call(bf16[8,8,2,64,512]{4,3,2,1,0:T(8,128)(2,1)} %bitcast.8, bf16[4,2,64,512]{3,2,1,0:T(8,128)(2,1)} %bitcast.10, bf16[1024,512]{1,0:T(8,128)(2,1)} %pad_maximum_fusion.4.cs_ref, bf16[1024,1024]{1,0:T(8,128)(2,1)} %get-tuple-element.23.ahead_ref, ...), custom_call_target="tpu_custom_call" | custom-call | tf_op jit(solution)/shard_map/convolve/pallas_call | solution.py:420
  467.1 2.4 bitcast_reduce_fusion
  469.4 0.0 all-reduce.2.cloned.1.call-update
  469.5 19.6 %unpack.1 = (bf16[64,32768]{1,0:T(8,128)(2,1)}, bf16[64,32768]{1,0:T(8,128)(2,1)}, bf16[64,32768]{1,0:T(8,128)(2,1)}, bf16[64,32768]{1,0:T(8,128)(2,1)}) custom-call(bf16[4,2,8,2,64,512]{5,4,3,2,1,0:T(8,128)(2,1)} %bitcast.9, bf16[64,32768]{1,0:T(8,128)(2,1)} %outer_ref.3, bf16[64,32768]{1,0:T(8,128)(2,1)} %inner_ref.3, bf16[64,32768]{1,0:T(8,128)(2,1)} %signal_ref.3, ...), custom_call_target="tpu_custom_call" | custom-call | tf_op jit(solution)/shard_map/unpack/pallas_call | solution.py:453
  489.1 12.9 %all-reduce.2.cloned.1.call-done = bf16[2,4,64,512]{3,2,0,1:T(8,128)(2,1)} async-done(((bf16[2,4,64,512]{3,2,0,1:T(8,128)(2,1)}), bf16[2,4,64,512]{3,2,0,1:T(8,128)(2,1)}) %all-reduce.2.cloned.1.call-update) | async-done | bytes 524304 | tf_op jit(solution)/shard_map/psum | solution.py:450
  502.0 2.1 copy.12
Async XLA Ops:
  7.2 494.8 %all-reduce.2.cloned.1.call-start = ((), (), s32[]{:S(2)}) async-start(), calls=%async_computation | async-start | bytes 1048576 | tf_op jit(solution)/shard_map/psum | solution.py:450
  21.5 11.1 %copy-start = (f32[2,4,64,512]{3,2,1,0:T(8,128)S(1)}, f32[2,4,64,512]{3,2,1,0:T(8,128)}, u32[]{:S(2)}) copy-start(f32[2,4,64,512]{3,2,1,0:T(8,128)} %param.8) | copy-start | bytes 3145732
Sparse Core Ops, SparseCore 0:
  469.6 32.3 all-reduce.1

commit v2 on v1

--- a/solution.py
+++ b/solution.py
@@ -3,6 +3,7 @@
 
 import jax
 import jax.numpy as jnp
+import numpy as np
 from jax import lax
 from jax.experimental import pallas as pl
 from jax.experimental.pallas import tpu as pltpu
@@ -178,8 +179,10 @@
     return (output, gradient_outer, gradient_inner, gradient_signal, gradient_filter)
 
 
-def channel_slots(channels, filters, devices):
-    if channels % devices or devices % filters:
+def channel_slots(channels, filters, devices, rows, lanes):
+    if channels % devices or devices % filters or devices % 2 or channels % 16 or 16 % filters:
+        return 0
+    if (channels // devices) % (16 // filters) or rows % (16 * lanes):
         return 0
     return devices // filters
 
@@ -216,6 +219,7 @@
 
 def convolve_kernel(
     devices,
+    lanes,
     shares,
     send_ref,
     taps_ref,
@@ -232,6 +236,11 @@
     taps,
     grads,
     grads_sent,
+    parts,
+    quarter,
+    arrived,
+    merged,
+    total,
     straight,
     filtered,
     unwound,
@@ -241,14 +250,52 @@
     back_recv_sems,
     small_send_sems,
     small_recv_sems,
+    lane_send_sems,
+    lane_recv_sems,
 ):
     me = lax.axis_index("seq")
+    lane = lax.axis_index("chan")
     count, rows, factor = send_ref.shape[1], send_ref.shape[3], send_ref.shape[4]
     step = held.shape[0] // 2 * rows
     length = factor * factor
+    thin = rows // lanes
 
     def peer(offset):
         return lax.rem(me + offset, devices)
+
+    def lane_peer(offset):
+        return lax.rem(lane + offset, lanes)
+
+    def thin_rows(which):
+        return pl.ds(pl.multiple_of(which * thin, thin), thin)
+
+    def across(source, target, stage, offset):
+        if offset == 0:
+            return pltpu.make_async_copy(source, target, lane_recv_sems.at[stage, 0])
+        return pltpu.make_async_remote_copy(
+            src_ref=source,
+            dst_ref=target,
+            send_sem=lane_send_sems.at[stage, offset],
+            recv_sem=lane_recv_sems.at[stage, offset],
+            device_id={"chan": lane_peer(offset)},
+            device_id_type=MESH,
+        )
+
+    def taps_across(offset):
+        mine = taps.at[:, :, thin_rows(lane), :]
+        return across(mine, mine, 0, offset)
+
+    def parts_across(offset):
+        return across(grads_sent.at[:, :, thin_rows(lane_peer(offset)), :], parts.at[lane], 1, offset)
+
+    def merged_across(offset):
+        return across(merged, total.at[lane], 2, offset)
+
+    def arrive(make, offset):
+        if offset == 0:
+            make(offset).wait()
+        else:
+            make(offset).wait_recv()
 
     def copy(source, target, offset, send_sem, recv_sem):
         return pltpu.make_async_remote_copy(
@@ -276,49 +323,57 @@
         return copy(source, back_ref.at[me, c], offset, back_send_sems.at[offset, c], back_recv_sems.at[offset, c])
 
     def tap(offset):
-        source = taps_ref.at[peer(offset) // shares]
+        source = taps_ref.at[peer(offset) // shares, :, thin_rows(lane), :]
+        target = taps.at[me, :, thin_rows(lane), :]
         if offset == 0:
-            return own(source, taps.at[me], small_recv_sems.at[0, 0])
-        return copy(source, taps.at[me], offset, small_send_sems.at[0, offset], small_recv_sems.at[0, offset])
+            return own(source, target, small_recv_sems.at[0, 0])
+        return copy(source, target, offset, small_send_sems.at[0, offset], small_recv_sems.at[0, offset])
 
     def grad(offset):
-        source = grads_sent.at[peer(offset)]
+        source = quarter.at[peer(offset)]
         if offset == 0:
-            return own(source, grads_ref.at[me], small_recv_sems.at[1, 0])
-        return copy(source, grads_ref.at[me], offset, small_send_sems.at[1, offset], small_recv_sems.at[1, offset])
+            return own(source, arrived.at[me], small_recv_sems.at[1, 0])
+        return copy(source, arrived.at[me], offset, small_send_sems.at[1, offset], small_recv_sems.at[1, offset])
 
     order = [0] + [k for pair in zip(range(1, devices), range(devices - 1, 0, -1)) for k in pair][: devices - 1]
 
     barrier = pltpu.get_barrier_semaphore()
     for offset in range(1, devices):
         pl.semaphore_signal(barrier, inc=1, device_id={"seq": peer(offset)}, device_id_type=MESH)
-    pl.semaphore_wait(barrier, devices - 1)
-
+    for offset in range(1, lanes):
+        pl.semaphore_signal(barrier, inc=1, device_id={"chan": lane_peer(offset)}, device_id_type=MESH)
+    pl.semaphore_wait(barrier, devices + lanes - 2)
+
+    def start_all(make, first, end):
+        @pl.loop(first, end)
+        def _(c):
+            for offset in order:
+                make(offset, c).start()
+
+    marks = (count // 4, count * 5 // 8, count * 7 // 8)
     for offset in order:
         tap(offset).start()
+    start_all(forth, 0, marks[0])
+    for offset in order:
+        arrive(tap, offset)
+    for offset in range(1, lanes):
+        taps_across(offset).start()
+    start_all(forth, marks[0], count)
+    grads[...] = jnp.zeros_like(grads)
+    for offset in range(1, lanes):
+        taps_across(offset).wait_recv()
+
+    def dot(left, right):
+        return jnp.dot(left, right, preferred_element_type=jnp.float32)
 
     @pl.loop(0, count)
     def _(c):
+        @pl.when(c == count - 1)
+        def _():
+            start_all(back, 0, marks[0])
+
         for offset in order:
-            forth(offset, c).start()
-
-    grads[...] = jnp.zeros_like(grads)
-    for offset in order:
-        if offset == 0:
-            tap(offset).wait()
-        else:
-            tap(offset).wait_recv()
-
-    def dot(left, right):
-        return jnp.dot(left, right, preferred_element_type=jnp.float32)
-
-    @pl.loop(0, count)
-    def _(c):
-        for offset in order:
-            if offset == 0:
-                forth(offset, c).wait()
-            else:
-                forth(offset, c).wait_recv()
+            arrive(lambda o: forth(o, c), offset)
 
         @pl.loop(0, 2)
         def _(half):
@@ -356,20 +411,43 @@
         for which in range(2):
             values = (dot(last_ref[...], unwound[which]) * (1.0 / length)).astype(jnp.bfloat16)
             made[c, :, which] = values.reshape(devices, rows, factor)
-        for offset in order:
-            back(offset, c).start()
 
     for part in range(2):
         scaled = (grads[part] * (1.0 / length)).astype(jnp.bfloat16)
         grads_sent[:, part] = scaled.reshape(devices, rows, factor)
+    for offset in range(lanes):
+        parts_across(offset).start()
+    start_all(back, marks[0], marks[1])
+    for offset in range(lanes):
+        arrive(parts_across, offset)
+    summed = parts[0].astype(jnp.float32)
+    for which in range(1, lanes):
+        summed = summed + parts[which].astype(jnp.float32)
+    quarter[...] = summed.astype(jnp.bfloat16)
     for offset in order:
         grad(offset).start()
+    start_all(back, marks[1], marks[2])
     for offset in order:
-        if offset == 0:
-            grad(offset).wait()
-        else:
-            grad(offset).wait()
-            tap(offset).wait_send()
+        arrive(grad, offset)
+    for group in range(devices // shares):
+        summed = arrived[group * shares].astype(jnp.float32)
+        for which in range(1, shares):
+            summed = summed + arrived[group * shares + which].astype(jnp.float32)
+        merged[group] = summed.astype(jnp.bfloat16)
+    for offset in range(lanes):
+        merged_across(offset).start()
+    start_all(back, marks[2], count)
+    for offset in range(lanes):
+        arrive(merged_across, offset)
+    for which in range(lanes):
+        for part in range(2):
+            grads_ref[part, :, which * thin : (which + 1) * thin, :] = total[which, :, part].astype(jnp.float32)
+    for offset in range(1, lanes):
+        for make in (taps_across, parts_across, merged_across):
+            make(offset).wait_send()
+    for offset in range(1, devices):
+        for make in (tap, grad):
+            make(offset).wait_send()
 
     @pl.loop(0, count)
     def _(c):
@@ -381,12 +459,25 @@
                 back(offset, c).wait()
 
 
-def by_channels(devices, shares, outer_gate, inner_gate, signal, filter_spectrum, cotangent):
+def wave_constants(factor):
+    ordinal = np.arange(factor)
+    angles = (np.outer(ordinal, ordinal) % factor) * (2.0 * np.pi / factor)
+    cos_table, sin_table = np.cos(angles), np.sin(angles)
+    twists = np.outer(ordinal, ordinal) * (2.0 * np.pi / (factor * factor))
+    tables = (
+        np.concatenate([cos_table, sin_table], axis=0),
+        np.block([[cos_table, -sin_table], [sin_table, cos_table]]),
+        np.block([[cos_table, sin_table], [-sin_table, cos_table]]),
+        np.concatenate([cos_table, -sin_table], axis=1),
+    )
+    return [t.astype(jnp.bfloat16) for t in tables] + [f(twists).astype(np.float32) for f in (np.cos, np.sin)]
+
+
+def by_channels(devices, lanes, shares, outer_gate, inner_gate, signal, filter_spectrum, cotangent):
     channels, positions = signal.shape
     filters, factor = filter_spectrum.shape[1], filter_spectrum.shape[3]
     rows = positions // factor
     count = channels // devices
-    length = factor * factor
     block, depth = 16, 16
     per = block // filters
     split = count // per
@@ -407,23 +498,17 @@
         name="pack",
     )(outer_gate, inner_gate, signal, cotangent)
     send = send.reshape(devices, count, 2, rows, factor)
-    cos_table, sin_table = wave_tables(factor)
-    ordinal = jnp.arange(factor, dtype=jnp.int32)
-    wave_cos, wave_sin = twist_grid(ordinal, ordinal, length)
-    cs = jnp.concatenate([cos_table, sin_table], axis=0)
-    ahead = jnp.block([[cos_table, -sin_table], [sin_table, cos_table]])
-    behind = jnp.block([[cos_table, sin_table], [-sin_table, cos_table]])
-    last = jnp.concatenate([cos_table, -sin_table], axis=1)
     taps = filter_spectrum.astype(jnp.bfloat16).transpose(1, 0, 2, 3)
     anywhere = pl.BlockSpec(memory_space=pl.ANY)
     inside = pl.BlockSpec(memory_space=pltpu.VMEM)
-    back, grads = pl.pallas_call(
-        functools.partial(convolve_kernel, devices, shares),
+    thin = rows // lanes
+    back, gradient_filter = pl.pallas_call(
+        functools.partial(convolve_kernel, devices, lanes, shares),
         in_specs=[anywhere, anywhere] + [inside] * 6,
-        out_specs=[anywhere, anywhere],
+        out_specs=[anywhere, inside],
         out_shape=[
             jax.ShapeDtypeStruct((devices, count, 2, rows, factor), jnp.bfloat16),
-            jax.ShapeDtypeStruct((devices, 2, rows, factor), jnp.bfloat16),
+            jax.ShapeDtypeStruct(filter_spectrum.shape, jnp.float32),
         ],
         scratch_shapes=[
             pltpu.VMEM((devices, count, 2, rows, factor), jnp.bfloat16),
@@ -431,6 +516,11 @@
             pltpu.VMEM((devices, 2, rows, factor), jnp.bfloat16),
             pltpu.VMEM((2, factor, factor), jnp.float32),
             pltpu.VMEM((devices, 2, rows, factor), jnp.bfloat16),
+            pltpu.VMEM((lanes, devices, 2, thin, factor), jnp.bfloat16),
+            pltpu.VMEM((devices, 2, thin, factor), jnp.bfloat16),
+            pltpu.VMEM((devices, 2, thin, factor), jnp.bfloat16),
+            pltpu.VMEM((filters, 2, thin, factor), jnp.bfloat16),
+            pltpu.VMEM((lanes, filters, 2, thin, factor), jnp.bfloat16),
             pltpu.VMEM((2, factor // 2, 2 * factor), jnp.bfloat16),
             pltpu.VMEM((2, factor // 2, 2 * factor), jnp.bfloat16),
             pltpu.VMEM((2, 2 * factor, factor), jnp.bfloat16),
@@ -440,16 +530,14 @@
             pltpu.SemaphoreType.DMA((devices, count)),
             pltpu.SemaphoreType.DMA((2, devices)),
             pltpu.SemaphoreType.DMA((2, devices)),
+            pltpu.SemaphoreType.DMA((3, lanes)),
+            pltpu.SemaphoreType.DMA((3, lanes)),
         ],
         compiler_params=pltpu.CompilerParams(
             collective_id=0, has_side_effects=True, vmem_limit_bytes=VMEM_BYTES
         ),
         name="convolve",
-    )(send, taps, cs, ahead, behind, last, wave_cos, wave_sin)
-    shared = grads.astype(jnp.float32).reshape(filters, shares, 2, rows, factor).sum(axis=1)
-    gradient_filter = lax.psum(
-        shared.transpose(1, 0, 2, 3).astype(jnp.bfloat16), "chan"
-    ).astype(jnp.float32)
+    )(send, taps, *wave_constants(factor))
     outputs = pl.pallas_call(
         functools.partial(unpack_kernel, filters, depth),
         grid=grid,
@@ -462,10 +550,11 @@
     return (*outputs, gradient_filter)
 
 
-def local_program(devices, outer_gate, inner_gate, signal, filter_spectrum, cotangent):
+def local_program(devices, lanes, outer_gate, inner_gate, signal, filter_spectrum, cotangent):
     filters = filter_spectrum.shape[1]
-    shares = channel_slots(signal.shape[0], filters, devices)
-    program = functools.partial(by_channels, devices, shares) if shares else per_device
+    rows = signal.shape[1] // filter_spectrum.shape[3]
+    shares = channel_slots(signal.shape[0], filters, devices, rows, lanes)
+    program = functools.partial(by_channels, devices, lanes, shares) if shares else per_device
     return program(outer_gate, inner_gate, signal, filter_spectrum, cotangent)
 
 
@@ -485,5 +574,5 @@
         P(None, None, "seq", None),
     )
     return jax.shard_map(
-        functools.partial(local_program, mesh.shape["seq"]), mesh=mesh, in_specs=in_specs, out_specs=out_specs, check_vma=False
-    )
+        functools.partial(local_program, mesh.shape["seq"], mesh.shape["chan"]), mesh=mesh, in_specs=in_specs, out_specs=out_specs, check_vma=False
+    )

time: 512 us -> 425 us (0.83)
  Pallas kernels: 453 us -> 421 us
  other arithmetic: 27.7 us -> 0 us
  between operations: 14.1 us -> 0.65 us
  waiting for transfers between devices: 13 us -> 0 us
    pallas_call x1, Pallas kernels: 418 us -> 386 us  [by_channels(): pl.pallas_call(functools.partial(convolve_kernel, devices, lanes, shares)...]
    psum x1 -> x0, waiting for transfers between devices: 12.9 us -> none  [by_channels(): lax.psum(shared.transpose(1, 0, 2, 3).astype(jnp.bfloat16), 'chan')]
    concatenate x3 -> x0, other arithmetic: 12.1 us -> none  [the longest x1 9.96 us: by_channels(): behind = jnp.block([[cos_table, sin_table], [-sin_table, cos_table]])]
  transfers between devices with their start and end apart: 1 -> 0, of which waited for: 1 -> 0; matrix products, arithmetic and copies ran while one was open for 0% -> 0% of each run, Pallas kernels for 4% -> 0%
where the time goes in v2:
time: 425 us; the launch traced here: 424 us
  Pallas kernels  421 us (99%)
    pallas_call x1, Pallas kernels, by_channels(): pl.pallas_call(functools.partial(convolve_kernel, devices, lanes, shares)...  386 us
    pallas_call x1, Pallas kernels, by_channels(): pl.pallas_call(functools.partial(unpack_kernel, filters, depth), grid=gri...  19.6 us
    pallas_call x1, Pallas kernels, by_channels(): pl.pallas_call(functools.partial(pack_kernel, filters, depth), grid=grid,...  15.4 us

profile of v2, /device:TPU:0, one launch (start us, length us, event | category | flops | bytes accessed | tf_op | source)
XLA Modules:
  0.0 424.3 jit_solution(3658961484149377540)
XLA Ops:
  0.6 2.1 copy.20
  2.7 15.4 %pack.1 = bf16[4,2,8,2,64,512]{5,4,3,2,1,0:T(8,128)(2,1)} custom-call(bf16[64,32768]{1,0:T(8,128)(2,1)} %outer_ref.3, bf16[64,32768]{1,0:T(8,128)(2,1)} %inner_ref.3, bf16[64,32768]{1,0:T(8,128)(2,1)} %signal_ref.3, bf16[64,32768]{1,0:T(8,128)(2,1)} %cotangent_ref.3), custom_call_target="tpu_custom_call" | custom-call | tf_op jit(solution)/shard_map/pack/pallas_call | solution.py:491
  18.1 385.5 %convolve.1 = (bf16[8,8,2,64,512]{4,3,2,1,0:T(8,128)(2,1)}, f32[2,4,64,512]{3,2,1,0:T(8,128)}) custom-call(bf16[8,8,2,64,512]{4,3,2,1,0:T(8,128)(2,1)} %bitcast.5, bf16[4,2,64,512]{3,2,1,0:T(8,128)(2,1)} %bitcast.7, bf16[1024,512]{1,0:T(8,128)(2,1)} %constant.12.clone.cs_ref, bf16[1024,1024]{1,0:T(8,128)(2,1)} %constant.13.clone.ahead_ref, ...), custom_call_target="tpu_custom_call" | custom-call | tf_op jit(solution)/shard_map/convolve/pallas_call | solution.py:505
  403.7 0.0 copy-start
  403.7 19.6 %unpack.1 = (bf16[64,32768]{1,0:T(8,128)(2,1)}, bf16[64,32768]{1,0:T(8,128)(2,1)}, bf16[64,32768]{1,0:T(8,128)(2,1)}, bf16[64,32768]{1,0:T(8,128)(2,1)}) custom-call(bf16[4,2,8,2,64,512]{5,4,3,2,1,0:T(8,128)(2,1)} %bitcast.6, bf16[64,32768]{1,0:T(8,128)(2,1)} %outer_ref.3, bf16[64,32768]{1,0:T(8,128)(2,1)} %inner_ref.3, bf16[64,32768]{1,0:T(8,128)(2,1)} %signal_ref.3, ...), custom_call_target="tpu_custom_call" | custom-call | tf_op jit(solution)/shard_map/unpack/pallas_call | solution.py:541
  423.3 0.0 copy-done
  423.3 1.0 copy.22
Async XLA Ops:
  403.7 19.6 %copy-start = (f32[2,4,64,512]{3,2,1,0:T(8,128)S(1)}, f32[2,4,64,512]{3,2,1,0:T(8,128)}, u32[]{:S(2)}) copy-start(f32[2,4,64,512]{3,2,1,0:T(8,128)} %get-tuple-element.26) | copy-start | bytes 3145732

commit v3 on v2

--- a/solution.py
+++ b/solution.py
@@ -223,12 +223,12 @@
     shares,
     send_ref,
     taps_ref,
-    cs_ref,
-    ahead_ref,
-    behind_ref,
-    last_ref,
-    wave_cos_ref,
-    wave_sin_ref,
+    cs_far,
+    ahead_far,
+    behind_far,
+    last_far,
+    wave_cos_far,
+    wave_sin_far,
     back_ref,
     grads_ref,
     held,
@@ -252,6 +252,13 @@
     small_recv_sems,
     lane_send_sems,
     lane_recv_sems,
+    cs_ref,
+    ahead_ref,
+    behind_ref,
+    last_ref,
+    wave_cos_ref,
+    wave_sin_ref,
+    table_sems,
 ):
     me = lax.axis_index("seq")
     lane = lax.axis_index("chan")
@@ -354,6 +361,11 @@
     for offset in order:
         tap(offset).start()
     start_all(forth, 0, marks[0])
+    far = (cs_far, ahead_far, behind_far, last_far, wave_cos_far, wave_sin_far)
+    near = (cs_ref, ahead_ref, behind_ref, last_ref, wave_cos_ref, wave_sin_ref)
+    tables = [own(source, target, table_sems.at[k]) for k, (source, target) in enumerate(zip(far, near))]
+    for table in tables:
+        table.start()
     for offset in order:
         arrive(tap, offset)
     for offset in range(1, lanes):
@@ -362,13 +374,15 @@
     grads[...] = jnp.zeros_like(grads)
     for offset in range(1, lanes):
         taps_across(offset).wait_recv()
+    for table in tables:
+        table.wait()
 
     def dot(left, right):
         return jnp.dot(left, right, preferred_element_type=jnp.float32)
 
     @pl.loop(0, count)
     def _(c):
-        @pl.when(c == count - 1)
+        @pl.when(c == max(count - 2, marks[0]))
         def _():
             start_all(back, 0, marks[0])
 
@@ -502,9 +516,10 @@
     anywhere = pl.BlockSpec(memory_space=pl.ANY)
     inside = pl.BlockSpec(memory_space=pltpu.VMEM)
     thin = rows // lanes
+    tables = wave_constants(factor)
     back, gradient_filter = pl.pallas_call(
         functools.partial(convolve_kernel, devices, lanes, shares),
-        in_specs=[anywhere, anywhere] + [inside] * 6,
+        in_specs=[anywhere] * 8,
         out_specs=[anywhere, inside],
         out_shape=[
             jax.ShapeDtypeStruct((devices, count, 2, rows, factor), jnp.bfloat16),
@@ -532,12 +547,14 @@
             pltpu.SemaphoreType.DMA((2, devices)),
             pltpu.SemaphoreType.DMA((3, lanes)),
             pltpu.SemaphoreType.DMA((3, lanes)),
+            *[pltpu.VMEM(table.shape, table.dtype) for table in tables],
+            pltpu.SemaphoreType.DMA((len(tables),)),
         ],
         compiler_params=pltpu.CompilerParams(
             collective_id=0, has_side_effects=True, vmem_limit_bytes=VMEM_BYTES
         ),
         name="convolve",
-    )(send, taps, *wave_constants(factor))
+    )(send, taps, *tables)
     outputs = pl.pallas_call(
         functools.partial(unpack_kernel, filters, depth),
         grid=grid,

time: 425 us -> 422 us (level)
  no operation moved by 1% of the time
where the time goes in v3:
time: 422 us; the launch traced here: 421 us
  Pallas kernels  417 us (99%)
    pallas_call x1, Pallas kernels, by_channels(): pl.pallas_call(functools.partial(convolve_kernel, devices, lanes, shares)...  382 us
    pallas_call x1, Pallas kernels, by_channels(): pl.pallas_call(functools.partial(unpack_kernel, filters, depth), grid=gri...  19.6 us
    pallas_call x1, Pallas kernels, by_channels(): pl.pallas_call(functools.partial(pack_kernel, filters, depth), grid=grid,...  15.4 us

profile of v3, /device:TPU:0, one launch (start us, length us, event | category | flops | bytes accessed | tf_op | source)
XLA Modules:
  0.0 420.9 jit_solution(1634530207799827231)
XLA Ops:
  0.6 2.1 copy.20
  2.7 15.4 %pack.1 = bf16[4,2,8,2,64,512]{5,4,3,2,1,0:T(8,128)(2,1)} custom-call(bf16[64,32768]{1,0:T(8,128)(2,1)} %outer_ref.3, bf16[64,32768]{1,0:T(8,128)(2,1)} %inner_ref.3, bf16[64,32768]{1,0:T(8,128)(2,1)} %signal_ref.3, bf16[64,32768]{1,0:T(8,128)(2,1)} %cotangent_ref.3), custom_call_target="tpu_custom_call" | custom-call | tf_op jit(solution)/shard_map/pack/pallas_call | solution.py:505
  18.1 382.1 %convolve.1 = (bf16[8,8,2,64,512]{4,3,2,1,0:T(8,128)(2,1)}, f32[2,4,64,512]{3,2,1,0:T(8,128)}) custom-call(bf16[8,8,2,64,512]{4,3,2,1,0:T(8,128)(2,1)} %bitcast.5, bf16[4,2,64,512]{3,2,1,0:T(8,128)(2,1)} %bitcast.7, bf16[1024,512]{1,0:T(8,128)(2,1)} %constant.12.clone.cs_far, bf16[1024,1024]{1,0:T(8,128)(2,1)} %constant.13.clone.ahead_far, ...), custom_call_target="tpu_custom_call" | custom-call | tf_op jit(solution)/shard_map/convolve/pallas_call | solution.py:520
  400.3 0.0 copy-start
  400.3 19.6 %unpack.1 = (bf16[64,32768]{1,0:T(8,128)(2,1)}, bf16[64,32768]{1,0:T(8,128)(2,1)}, bf16[64,32768]{1,0:T(8,128)(2,1)}, bf16[64,32768]{1,0:T(8,128)(2,1)}) custom-call(bf16[4,2,8,2,64,512]{5,4,3,2,1,0:T(8,128)(2,1)} %bitcast.6, bf16[64,32768]{1,0:T(8,128)(2,1)} %outer_ref.3, bf16[64,32768]{1,0:T(8,128)(2,1)} %inner_ref.3, bf16[64,32768]{1,0:T(8,128)(2,1)} %signal_ref.3, ...), custom_call_target="tpu_custom_call" | custom-call | tf_op jit(solution)/shard_map/unpack/pallas_call | solution.py:558
  419.9 0.0 copy-done
  419.9 1.0 copy.22
Async XLA Ops:
  400.3 19.6 %copy-start = (f32[2,4,64,512]{3,2,1,0:T(8,128)S(1)}, f32[2,4,64,512]{3,2,1,0:T(8,128)}, u32[]{:S(2)}) copy-start(f32[2,4,64,512]{3,2,1,0:T(8,128)} %get-tuple-element.26) | copy-start | bytes 3145732
